TPU v7x, 256 devices: a whole 4x4x8 slice. The times are simulated.
256 devices in a mesh: gx: 8 (over x, z_hi), gy: 8 (over y, core), gz: 4 (over z_lo).
Axes of the slice: x: 4, y: 4, z: 8 (z_hi: 2, z_lo: 4; z = z_hi * 4 + z_lo), core: 2. Of those that a mesh axis runs over, the one named last changes fastest.
Arguments:
- tokens: bfloat16 [1536, 4096], P(('gx', 'gy'), 'gz'), may hold values from -6 to 6
- gate_weight: bfloat16 [4096, 16384], P('gz', ('gx', 'gy')), may hold values from -0.09375 to 0.09375
- up_weight: bfloat16 [4096, 16384], P('gz', ('gx', 'gy')), may hold values from -0.09375 to 0.09375
- down_weight: bfloat16 [4096, 16384], P('gz', ('gx', 'gy')), may hold values from -0.046875 to 0.046875
- grad_out: bfloat16 [1536, 4096], P(('gx', 'gy'), 'gz'), may hold values from -6 to 6
Outputs:
- block_out: bfloat16 [1536, 4096], P(('gx', 'gy'), 'gz')
- grad_tokens: bfloat16 [1536, 4096], P(('gx', 'gy'), 'gz')
- grad_gate: float32 [4096, 16384], P('gz', ('gx', 'gy'))
- grad_up: float32 [4096, 16384], P('gz', ('gx', 'gy'))
- grad_down: float32 [4096, 16384], P('gz', ('gx', 'gy'))
All inputs are finite; a program needn't handle non-finite values.
Results may differ from a plain program's by a relative error of at most 0.013.
Values may be sent and summed in bfloat16 or wider, within the bound.
A program may use at most 128 MiB of HBM per device.

v0:
```python
import jax
import jax.numpy as jnp
from jax import lax
from jax.sharding import PartitionSpec as P


def rows_by_rows(left, right):
    return lax.dot_general(
        left, right, (((1,), (1,)), ((), ())), preferred_element_type=jnp.float32
    )


def cols_by_cols(left, right):
    return lax.dot_general(
        left, right, (((0,), (0,)), ((), ())), preferred_element_type=jnp.float32
    )


def all_rows(values):
    return lax.all_gather(values, ("gx", "gy"), axis=0, tiled=True)


def unit_total(members):
    return lax.psum(members, "gz")


def activate(gate_sum, up_sum):
    sigmoid_gate = 1.0 / (1.0 + jnp.exp(-gate_sum))
    return (gate_sum * sigmoid_gate * up_sum).astype(jnp.bfloat16)


def local_grads(hidden_grad, gate_sum, up_sum):
    sigmoid_gate = 1.0 / (1.0 + jnp.exp(-gate_sum))
    silu_gate = gate_sum * sigmoid_gate
    gate_grad = (
        hidden_grad * up_sum * sigmoid_gate * (1.0 + gate_sum * (1.0 - sigmoid_gate))
    ).astype(jnp.bfloat16)
    up_part_grad = (hidden_grad * silu_gate).astype(jnp.bfloat16)
    return (gate_grad, up_part_grad)


def forward_units(gate_part, up_part):
    gate_sum, up_sum = unit_total((gate_part, up_part))
    hidden = activate(gate_sum, up_sum)
    return (hidden, gate_sum, up_sum)


def backward_units(hidden_part, gate_sum, up_sum):
    (hidden_grad,) = unit_total((hidden_part,))
    gate_grad, up_part_grad = local_grads(hidden_grad, gate_sum, up_sum)
    return (gate_grad, up_part_grad)


def spread_sum(term_fn, own_rows):
    return lax.psum_scatter(
        term_fn(jnp.int32(0), own_rows * lax.axis_size(("gx", "gy"))),
        ("gx", "gy"),
        scatter_dimension=0,
        tiled=True,
    )


def on_device(tokens, gate_weight, up_weight, down_weight, grad_out):
    own_rows = tokens.shape[0]
    tokens_all = all_rows(tokens)
    gate_part = jnp.dot(tokens_all, gate_weight, preferred_element_type=jnp.float32)
    up_part = jnp.dot(tokens_all, up_weight, preferred_element_type=jnp.float32)
    hidden, gate_sum, up_sum = forward_units(gate_part, up_part)

    def out_term(begin_row, row_count):
        return rows_by_rows(hidden, down_weight)

    projected = spread_sum(out_term, own_rows)
    block_out = (tokens.astype(jnp.float32) + projected).astype(jnp.bfloat16)
    grads_all = all_rows(grad_out)
    hidden_part = jnp.dot(grads_all, down_weight, preferred_element_type=jnp.float32)
    gate_grad, up_part_grad = backward_units(hidden_part, gate_sum, up_sum)

    def back_term(begin_row, row_count):
        return rows_by_rows(gate_grad, gate_weight) + rows_by_rows(up_part_grad, up_weight)

    backward = spread_sum(back_term, own_rows)
    grad_tokens = (grad_out.astype(jnp.float32) + backward).astype(jnp.bfloat16)
    grad_gate = cols_by_cols(tokens_all, gate_grad)
    grad_up = cols_by_cols(tokens_all, up_part_grad)
    grad_down = cols_by_cols(grads_all, hidden)
    return (block_out, grad_tokens, grad_gate, grad_up, grad_down)


def solution(mesh):
    in_specs = (
        P(("gx", "gy"), "gz"),
        P("gz", ("gx", "gy")),
        P("gz", ("gx", "gy")),
        P("gz", ("gx", "gy")),
        P(("gx", "gy"), "gz"),
    )
    out_specs = (
        P(("gx", "gy"), "gz"),
        P(("gx", "gy"), "gz"),
        P("gz", ("gx", "gy")),
        P("gz", ("gx", "gy")),
        P("gz", ("gx", "gy")),
    )
    return jax.shard_map(
        on_device, mesh=mesh, in_specs=in_specs, out_specs=out_specs, check_vma=False
    )
```

profile of v0, /device:TPU:1, one launch (start us, length us, event | category | flops | bytes accessed | tf_op | source)
XLA Modules:
  0.0 748.5 jit_solution(9589761963290921756)
XLA Ops:
  7.2 0.0 copy-start
  7.2 0.0 all-gather.3.cloned.1.call-start
  7.2 0.7 all-gather.3.cloned.1.call-update
  7.9 0.0 all-gather.5.cloned.1.call-start
  8.0 0.7 all-gather.5.cloned.1.call-update
  8.7 0.0 all-reduce.3.cloned.1.call-start
  8.7 94.7 %all-gather.3.cloned.1.call-done = bf16[1536,1024]{1,0:T(8,128)(2,1)} async-done(((bf16[24,1024]{1,0:T(8,128)(2,1)}), bf16[1536,1024]{1,0:T(8,128)(2,1)}) %all-gather.3.cloned.1.call-update) | async-done | bytes 3145744 | tf_op jit(solution)/shard_map/all_gather | solution.py:20
  103.4 0.0 copy-start.5
  103.4 4.3 fusion.2
  107.7 0.0 copy-done
  107.7 0.0 copy-done.5
  107.7 0.0 copy-start.1
  107.7 2.1 fusion.1
  109.8 78.5 %all-gather.5.cloned.1.call-done = bf16[1536,1024]{1,0:T(8,128)(2,1)} async-done(((bf16[24,1024]{1,0:T(8,128)(2,1)}), bf16[1536,1024]{1,0:T(8,128)(2,1)}) %all-gather.5.cloned.1.call-update) | async-done | bytes 3145744 | tf_op jit(solution)/shard_map/all_gather | solution.py:20
  188.4 0.0 copy-done.1
  188.4 4.1 fusion.4
  192.5 0.0 all-reduce.3.cloned.1.call-update
  192.5 0.0 reduce-scatter.5.cloned.1.call-start
  192.6 175.9 %all-reduce.3.cloned.1.call-done = (f32[1536,256]{1,0:T(8,128)}, f32[1536,256]{1,0:T(8,128)}, f32[1536,256]{1,0:T(8,128)}) async-done(((f32[1536,256]{1,0:T(8,128)}, f32[1536,256]{1,0:T(8,128)}, f32[1536,256]{1,0:T(8,128)}), (f32[1536,256]{1,0:T(8,128)}, f32[1536,256]{1,0:T(8,128)}, f32[1536,256]{1,0:T(8,128)})) %all-reduce.3.cloned.1.call-update) | async-done | bytes 4718608 | tf_op jit(solution)/shard_map/psum | solution.py:24
  368.5 3.2 multiply_convert_fusion
  371.7 0.0 copy-start.2
  371.7 1.0 fusion.5
  372.7 0.0 copy-done.2
  372.7 3.7 convolution_add_fusion
  376.4 0.0 reduce-scatter.5.cloned.1.call-update
  376.4 0.0 reduce-scatter.3.cloned.1.call-start
  376.5 3.7 fusion.3
  380.1 0.0 reduce-scatter.3.cloned.1.call-update
  380.1 3.9 convolution_bitcast_fusion
  384.0 2.5 copy.12
  386.5 2.9 convolution_bitcast_fusion.2
  389.5 1.3 copy.10
  390.8 0.0 copy-start.3
  390.8 0.0 copy-start.4
  390.8 3.0 convolution_bitcast_fusion.1
  393.8 1.3 copy.11
  395.1 162.2 %reduce-scatter.5.cloned.1.call-done = f32[24,1024]{1,0:T(8,128)} async-done(((f32[1536,1024]{1,0:T(8,128)}), f32[24,1024]{1,0:T(8,128)}) %reduce-scatter.5.cloned.1.call-update) | async-done | bytes 98320 | tf_op jit(solution)/shard_map/reduce_scatter | solution.py:55
  557.3 0.0 copy-done.3
  557.3 1.5 add_convert_fusion
  558.8 181.7 %reduce-scatter.3.cloned.1.call-done = f32[24,1024]{1,0:T(8,128)} async-done(((f32[1536,1024]{1,0:T(8,128)}), f32[24,1024]{1,0:T(8,128)}) %reduce-scatter.3.cloned.1.call-update) | async-done | bytes 98320 | tf_op jit(solution)/shard_map/reduce_scatter | solution.py:55
  740.5 0.0 copy-done.4
  740.5 1.5 add_convert_fusion.1
Async XLA Ops:
  7.2 100.5 %copy-start = (bf16[1024,256]{1,0:T(8,128)(2,1)S(1)}, bf16[1024,256]{1,0:T(8,128)(2,1)}, u32[]{:S(2)}) copy-start(bf16[1024,256]{1,0:T(8,128)(2,1)} %param.6) | copy-start | bytes 1572868
  7.2 96.2 %all-gather.3.cloned.1.call-start = ((), (), s32[]{:S(2)}) async-start(), calls=%async_computation.2 | async-start | bytes 3194880 | tf_op jit(solution)/shard_map/all_gather | solution.py:20
  7.9 180.5 %all-gather.5.cloned.1.call-start = ((), (), s32[]{:S(2)}) async-start(), calls=%async_computation.4 | async-start | bytes 3194880 | tf_op jit(solution)/shard_map/all_gather | solution.py:20
  8.7 359.8 %all-reduce.3.cloned.1.call-start = ((), (), s32[]{:S(2)}) async-start(), calls=%async_computation.6 | async-start | bytes 9437184 | tf_op jit(solution)/shard_map/psum | solution.py:24
  103.4 4.3 copy-start.5
  107.7 80.7 %copy-start.1 = (bf16[1024,256]{1,0:T(8,128)(2,1)S(1)}, bf16[1024,256]{1,0:T(8,128)(2,1)}, u32[]{:S(2)}) copy-start(bf16[1024,256]{1,0:T(8,128)(2,1)} %param.8) | copy-start | bytes 1572868
  192.5 364.7 %reduce-scatter.5.cloned.1.call-start = ((), (), s32[]{:S(2)}) async-start(), calls=%async_computation.5 | async-start | bytes 6389760 | tf_op jit(solution)/shard_map/reduce_scatter | solution.py:55
  371.7 1.0 copy-start.2
  376.4 364.1 %reduce-scatter.3.cloned.1.call-start = ((), (), s32[]{:S(2)}) async-start(), calls=%async_computation.3 | async-start | bytes 6389760 | tf_op jit(solution)/shard_map/reduce_scatter | solution.py:55
  390.8 166.5 %copy-start.3 = (bf16[24,1024]{1,0:T(8,128)(2,1)S(1)}, bf16[24,1024]{1,0:T(8,128)(2,1)}, u32[]{:S(2)}) copy-start(bf16[24,1024]{1,0:T(8,128)(2,1)} %param.9) | copy-start | bytes 147460
  390.8 349.7 %copy-start.4 = (bf16[24,1024]{1,0:T(8,128)(2,1)S(1)}, bf16[24,1024]{1,0:T(8,128)(2,1)}, u32[]{:S(2)}) copy-start(bf16[24,1024]{1,0:T(8,128)(2,1)} %param.5) | copy-start | bytes 147460
Sparse Core Ops, SparseCore 0:
  11.7 91.6 all-gather.2
  107.0 81.2 all-gather.4
  192.6 175.7 all-reduce.2
  376.5 180.6 reduce-scatter.4
  563.9 176.5 reduce-scatter.2
where the time goes:
time: 749 us
  waiting for transfers between devices  694 us (93%)
  matrix products  28.7 us (4%)
  between operations  13.8 us (2%)
    reduce_scatter x2, waiting for transfers between devices, spread_sum(): lax.psum_scatter(term_fn(jnp.int32(0), own_rows * lax.axis_size(('gx', 'g...  344 us
    psum x1, waiting for transfers between devices, unit_total(): return lax.psum(members, 'gz')  176 us
    all_gather x2, waiting for transfers between devices, all_rows(): return lax.all_gather(values, ('gx', 'gy'), axis=0, tiled=True)  173 us
  transfers between devices with their start and end apart: 5, of which 5 were waited for; matrix products, arithmetic and copies ran while one was open for 4% of the time, Pallas kernels for 0%

commit v1 on v0

v1 whole, which is shorter than its diff:
```python
import functools

import jax
import jax.numpy as jnp
from jax import lax
from jax.experimental import pallas as pl
from jax.experimental.pallas import tpu as pltpu
from jax.sharding import PartitionSpec as P

MESH = pl.DeviceIdType.MESH
F32 = jnp.float32
BF16 = jnp.bfloat16
CHUNKS = 8


def chunk_place(k):
    pair, odd = k // 2, k % 2
    first = 1 - (pair + 2) // 3
    last = pair // 3
    third = pair // 2 - last
    dzh = first * odd + third + last * (1 - odd)
    dy = (1 - first - last) * (1 + 2 * odd) + 2 * last
    return dzh, dy


def dot_nn(a, b):
    return jnp.dot(a, b, preferred_element_type=F32)


def dot_nt(a, b):
    return lax.dot_general(a, b, (((1,), (1,)), ((), ())), preferred_element_type=F32)


def dot_tn(a, b):
    return lax.dot_general(a, b, (((0,), (0,)), ((), ())), preferred_element_type=F32)


def body(
    tok, grd, wg_any, wu_any, wd_any,
    out, gtok, d_gate, d_up, d_down,
    wg, wu, wd, mine, theirs, gath, part, zsend, zin1, zin2, res,
    both, cin, xsend, xin, ysend, yin, zhs, zhin, fin, fin_in,
    w_sem, cx, zx, xa, ya, fw, z1, z2, z3, co, xr, yr, zr, fo,
):
    gx, gy, zl = lax.axis_index("gx"), lax.axis_index("gy"), lax.axis_index("gz")
    x, zh, y, c = gx // 2, gx % 2, gy // 2, gy % 2
    units = wg.shape[1]
    feats = wg.shape[0]
    rows = gath.shape[2] * gath.shape[3]

    def at(x_, zh_, y_, c_, zl_):
        return (x_ * 2 + zh_, y_ * 2 + c_, zl_)

    def x_peer(j):
        return at((x + j) % 4, zh, y, c, zl)

    def y_peer(j):
        return at(x, zh, (y + j) % 4, c, zl)

    core_peer = at(x, zh, y, 1 - c, zl)
    half_peer = at(x, 1 - zh, y, c, zl)
    pair_z = zl + 1 - 2 * (zl % 2)
    pair_peer = at(x, zh, y, c, pair_z)
    mid_peer = at(x, zh, y, c, 3 - zl)
    is_mid = ((zl + 1) // 2) % 2 == 1
    is_end = ((zl + 1) // 2) % 2 == 0

    def send(src, dst, sems, idx, peer):
        return pltpu.make_async_remote_copy(
            src_ref=src, dst_ref=dst, send_sem=sems.at[(0, *idx)], recv_sem=sems.at[(1, *idx)],
            device_id=peer, device_id_type=MESH,
        )

    def slot(k):
        dzh, dy = chunk_place(k)
        return ((zh + dzh) % 2) * 4 + (y + dy) % 4

    def core_copy():
        return send(mine, theirs, cx, (0,), core_peer)

    def half_copy(place):
        return send(gath.at[c, place, x], gath.at[c, place, x], zx, (0,), half_peer)

    def gather_x(dzh, j, owner):
        place = ((zh + dzh) % 2) * 4 + y
        return send(gath.at[c, place, owner], gath.at[c, place, owner], xa, (dzh, j - 1), x_peer(-j))

    def gather_y(k, place, dy):
        return send(gath.at[c, place], gath.at[c, place], ya, (k,), y_peer(4 - dy))

    def forward(k, which):
        return send(gath.at[which, slot(k)], gath.at[which, slot(k)], fw, (k,), core_peer)

    def to_pair(k):
        return send(zsend.at[k], zin1.at[k], z1, (k,), pair_peer)

    def to_mid(k):
        return send(zsend.at[k], zin2.at[k], z2, (k,), mid_peer)

    def to_end(k):
        return send(res.at[k], res.at[k], z3, (k,), pair_peer)

    def to_core(k):
        return send(both.at[k, 1 - c], cin.at[k], co, (k,), core_peer)

    def scatter_x(k, j):
        return send(xsend.at[k, (x + j) % 4], xin.at[k, j - 1], xr, (k, j - 1), x_peer(j))

    def scatter_y(k):
        _, dy = chunk_place(k)
        return send(ysend.at[k], yin.at[k], yr, (k,), y_peer(dy))

    def half_back():
        return send(zhs, zhin, zr, (0,), half_peer)

    def last_copy():
        return send(fin, fin_in, fo, (0,), core_peer)

    weight_copies = [
        pltpu.make_async_copy(src, dst, w_sem.at[n])
        for n, (src, dst) in enumerate(((wg_any, wg), (wu_any, wu), (wd_any, wd)))
    ]
    for cp in weight_copies:
        cp.start()

    peers = [core_peer, half_peer, pair_peer, mid_peer]
    peers += [x_peer(j) for j in (1, 2, 3)] + [y_peer(j) for j in (1, 2, 3)]
    barrier = pltpu.get_barrier_semaphore()
    for peer in peers:
        pl.semaphore_signal(barrier, inc=1, device_id=peer, device_id_type=MESH)
    mine[...] = jnp.concatenate([tok[...].astype(F32), grd[...].astype(F32)], axis=0).astype(BF16)
    pl.semaphore_wait(barrier, len(peers))

    core_copy().start()
    core_copy().wait_recv()
    m, t = mine[...].astype(F32), theirs[...].astype(F32)
    half = m.shape[0] // 2
    lo = jnp.where(c == 0, m[:half], t[half:])
    hi = jnp.where(c == 0, t[:half], m[half:])
    own = zh * 4 + y
    other = (1 - zh) * 4 + y
    gath[c, own, x] = jnp.concatenate([lo, hi], axis=0).astype(BF16)
    half_copy(own).start()
    for j in (1, 3, 2):
        gather_x(0, j, x).start()
    d_gate[...] = jnp.zeros_like(d_gate)
    d_up[...] = jnp.zeros_like(d_up)
    d_down[...] = jnp.zeros_like(d_down)
    for cp in weight_copies:
        cp.wait()
    for j in (1, 3, 2):
        gather_x(0, j, (x + j) % 4).wait_recv()
    forward(0, c).start()

    def gather_send(k):
        dzh, dy = chunk_place(k)
        gather_y(k, ((zh + dzh) % 2) * 4 + y, dy).start()

    gather_send(2)
    gather_send(3)

    def stage_partial(k):
        forward(k, 1 - c).wait_recv()
        s = slot(k)
        xs = gath[0, s].reshape(rows, feats)
        ys = gath[1, s].reshape(rows, feats)
        for n, (a, w) in enumerate(((xs, wg), (xs, wu), (ys, wd))):
            p = dot_nn(a, w[...])
            part[k, n] = p
            zsend[k, n] = p.astype(BF16)

        @pl.when(is_end)
        def _():
            to_pair(k).start()

    def stage_forward(k):
        @pl.when(k == 1)
        def _():
            half_copy(other).wait_recv()
            for j in (1, 3, 2):
                gather_x(1, j, x).start()
            for j in (1, 3, 2):
                gather_x(1, j, (x + j) % 4).wait_recv()

        @pl.when(k >= 2)
        def _():
            gather_y(k, slot(k), 0).wait_recv()

        forward(k, c).start()

    def stage_pair(k):
        to_pair(k).wait_recv()
        for n in range(3):
            a = part[k, n] + zin1[k, n].astype(F32)
            part[k, n] = a
            zsend[k, n] = a.astype(BF16)
        to_mid(k).start()

    def stage_units(k):
        to_mid(k).wait_recv()
        g = part[k, 0] + zin2[k, 0].astype(F32)
        u = part[k, 1] + zin2[k, 1].astype(F32)
        h = part[k, 2] + zin2[k, 2].astype(F32)
        sig = 1.0 / (1.0 + jnp.exp(-g))
        silu = g * sig
        res[k, 0] = (silu * u).astype(BF16)
        res[k, 1] = (h * u * sig * (1.0 + g * (1.0 - sig))).astype(BF16)
        res[k, 2] = (h * silu).astype(BF16)
        to_end(k).start()

    def stage_project(k):
        @pl.when(is_end)
        def _():
            to_end(k).wait_recv()

        hid, gg, ug = res[k, 0], res[k, 1], res[k, 2]
        both[k, 0] = dot_nt(hid, wd[...]).astype(BF16).reshape(both.shape[2:])
        both[k, 1] = (dot_nt(gg, wg[...]) + dot_nt(ug, wu[...])).astype(BF16).reshape(both.shape[2:])
        to_core(k).start()

    def stage_weights(k):
        hid, gg, ug = res[k, 0], res[k, 1], res[k, 2]
        s = slot(k)
        xs = gath[0, s].reshape(rows, feats)
        ys = gath[1, s].reshape(rows, feats)
        d_gate[...] += dot_tn(xs, gg)
        d_up[...] += dot_tn(xs, ug)
        d_down[...] += dot_tn(ys, hid)

    def stage_core(k):
        to_core(k).wait_recv()
        xsend[k] = (both[k, c].astype(F32) + cin[k].astype(F32)).astype(BF16)
        for j in (1, 3, 2):
            scatter_x(k, j).start()

    def stage_x(k):
        for j in (1, 3, 2):
            scatter_x(k, j).wait_recv()
        s = xsend[k, x].astype(F32)
        for j in range(3):
            s += xin[k, j].astype(F32)
        ysend[k] = s.astype(BF16)

        @pl.when(k >= 2)
        def _():
            scatter_y(k).start()

    def step(i, _):
        def when(k, fn, cond=None):
            ok = (k >= 0) & (k < CHUNKS)
            pl.when(ok if cond is None else ok & cond)(lambda: fn(k))

        when(i - 9, stage_x)
        when(i - 7, stage_core)
        when(i - 6, stage_project)
        when(i - 4, stage_units, is_mid)
        when(i - 2, stage_pair, is_mid)
        when(i, stage_partial)
        when(i + 1, stage_forward)

        @pl.when(i == 0)
        def _():
            gather_send(4)
            gather_send(5)

        @pl.when(i == 2)
        def _():
            gather_send(6)
            gather_send(7)

        when(i - 6, stage_weights)
        return 0

    lax.fori_loop(0, CHUNKS + 9, step, 0)

    def total(first, others):
        s = ysend[first].astype(F32)
        for k in others:
            scatter_y(k).wait_recv()
            s += yin[k].astype(F32)
        return s

    zhs[...] = total(1, (4, 5, 6)).astype(BF16)
    half_back().start()
    s = total(0, (2, 3, 7))
    half_back().wait_recv()
    s += zhin[...].astype(F32)
    fin[...] = (gath[c, own, x].astype(F32) + s).astype(BF16)
    last_copy().start()
    last_copy().wait_recv()
    a, b = fin[...].astype(F32), fin_in[...].astype(F32)
    first = jnp.where(c == 0, a[:half], b[half:])
    second = jnp.where(c == 0, b[:half], a[half:])
    out[...] = first.astype(BF16)
    gtok[...] = second.astype(BF16)

    core_copy().wait_send()
    half_copy(own).wait_send()
    for dzh in (0, 1):
        for j in (1, 2, 3):
            gather_x(dzh, j, x).wait_send()

    def drain(k, _):
        @pl.when(k >= 2)
        def _():
            gather_y(k, slot(k), 0).wait_send()
            scatter_y(k).wait_send()

        forward(k, c).wait_send()

        @pl.when(is_end)
        def _():
            to_pair(k).wait_send()

        @pl.when(is_mid)
        def _():
            to_mid(k).wait_send()
            to_end(k).wait_send()

        to_core(k).wait_send()
        for j in (1, 2, 3):
            scatter_x(k, j).wait_send()
        return 0

    lax.fori_loop(0, CHUNKS, drain, 0)
    half_back().wait_send()
    last_copy().wait_send()


def on_device(tokens, gate_weight, up_weight, down_weight, grad_out):
    own_rows, feats = tokens.shape
    units = gate_weight.shape[1]
    block = 2 * own_rows
    rows = 4 * block
    dma = pltpu.SemaphoreType.DMA
    vm = pltpu.VMEM
    wshape = (feats, units)
    any_spec = pl.BlockSpec(memory_space=pl.ANY)
    vmem_spec = pl.BlockSpec(memory_space=pltpu.VMEM)
    return pl.pallas_call(
        body,
        out_shape=(
            jax.ShapeDtypeStruct(tokens.shape, BF16),
            jax.ShapeDtypeStruct(tokens.shape, BF16),
            jax.ShapeDtypeStruct(wshape, F32),
            jax.ShapeDtypeStruct(wshape, F32),
            jax.ShapeDtypeStruct(wshape, F32),
        ),
        in_specs=[vmem_spec, vmem_spec, any_spec, any_spec, any_spec],
        out_specs=[vmem_spec] * 5,
        scratch_shapes=[
            vm(wshape, BF16), vm(wshape, BF16), vm(wshape, BF16),
            vm((block, feats), BF16), vm((block, feats), BF16),
            vm((2, CHUNKS, 4, block, feats), BF16),
            vm((CHUNKS, 3, rows, units), F32),
            vm((CHUNKS, 3, rows, units), BF16),
            vm((CHUNKS, 3, rows, units), BF16),
            vm((CHUNKS, 3, rows, units), BF16),
            vm((CHUNKS, 3, rows, units), BF16),
            vm((CHUNKS, 2, 4, block, feats), BF16),
            vm((CHUNKS, 4, block, feats), BF16),
            vm((CHUNKS, 4, block, feats), BF16),
            vm((CHUNKS, 3, block, feats), BF16),
            vm((CHUNKS, block, feats), BF16),
            vm((CHUNKS, block, feats), BF16),
            vm((block, feats), BF16), vm((block, feats), BF16),
            vm((block, feats), BF16), vm((block, feats), BF16),
            dma((3,)),
            dma((2, 1)), dma((2, 1)), dma((2, 2, 3)), dma((2, CHUNKS)), dma((2, CHUNKS)),
            dma((2, CHUNKS)), dma((2, CHUNKS)), dma((2, CHUNKS)), dma((2, CHUNKS)),
            dma((2, CHUNKS, 3)), dma((2, CHUNKS)), dma((2, 1)), dma((2, 1)),
        ],
        compiler_params=pltpu.CompilerParams(
            collective_id=0, has_side_effects=True, vmem_limit_bytes=60 << 20
        ),
        cost_estimate=pl.CostEstimate(
            flops=18 * 8 * rows * feats * units,
            transcendentals=8 * rows * units,
            bytes_accessed=20 * feats * units,
        ),
        name="swiglu_block",
    )(tokens, grad_out, gate_weight, up_weight, down_weight)


def solution(mesh):
    rows_spec = P(("gx", "gy"), "gz")
    weight_spec = P("gz", ("gx", "gy"))
    return jax.shard_map(
        on_device,
        mesh=mesh,
        in_specs=(rows_spec, weight_spec, weight_spec, weight_spec, rows_spec),
        out_specs=(rows_spec, rows_spec, weight_spec, weight_spec, weight_spec),
        check_vma=False,
    )
```

time: 749 us -> 125 us (0.17)
  waiting for transfers between devices: 694 us -> 0 us
  Pallas kernels: 0 us -> 118 us
  matrix products: 28.7 us -> 0 us
  between operations: 13.8 us -> 0.65 us
    reduce_scatter x2 -> x0, waiting for transfers between devices: 344 us -> none  [spread_sum(): lax.psum_scatter(term_fn(jnp.int32(0), own_rows * lax.axis_size(('gx', 'g...]
    psum x1 -> x0, waiting for transfers between devices: 176 us -> none  [unit_total(): return lax.psum(members, 'gz')]
    all_gather x2 -> x0, waiting for transfers between devices: 173 us -> none  [all_rows(): return lax.all_gather(values, ('gx', 'gy'), axis=0, tiled=True)]
    pallas_call x0 -> x1, Pallas kernels: none -> 118 us  [on_device(): pl.pallas_call(body, out_shape=(jax.ShapeDtypeStruct(tokens.shape, BF16),...]
    dot_general x9 -> x0, matrix products: 28.7 us -> none  [the longest x3 9.76 us: cols_by_cols(): lax.dot_general(left, right, (((0,), (0,)), ((), ())), preferred_element_...]
  transfers between devices with their start and end apart: 5 -> 0, of which waited for: 5 -> 0; matrix products, arithmetic and copies ran while one was open for 4% -> 0% of each run, Pallas kernels for 0% -> 0%
where the time goes in v1:
time: 125 us
  Pallas kernels  118 us (94%)
  local copies, waits for them, and re-layouts  6.98 us (6%)
    pallas_call x1, Pallas kernels, on_device(): pl.pallas_call(body, out_shape=(jax.ShapeDtypeStruct(tokens.shape, BF16),...  118 us
    unnamed x11, local copies, waits for them, and re-layouts  6.98 us

profile of v1, /device:TPU:1, one launch (start us, length us, event | category | flops | bytes accessed | tf_op | source)
XLA Modules:
  0.0 125.1 jit_solution(6688935438810797844)
XLA Ops:
  0.6 117.5 %swiglu_block.1 = (bf16[24,1024]{1,0:T(8,128)(2,1)}, bf16[24,1024]{1,0:T(8,128)(2,1)}, f32[1024,256]{1,0:T(8,128)}, f32[1024,256]{1,0:T(8,128)}, f32[1024,256]{1,0:T(8,128)}) custom-call(bf16[24,1024]{1,0:T(8,128)(2,1)} %tok.1, bf16[24,1024]{1,0:T(8,128)(2,1)} %grd.1, bf16[1024,256]{1,0:T(8,128)(2,1)} %wg_any.1, bf16[1024,256]{1,0:T(8,128)(2,1)} %wu_any.1, ...), custom_call_target="tpu_custom_call" | custom-call | flops 7247757312 | bytes 5242880 | tf_op jit(solution)/shard_map/swiglu_block/pallas_call | solution.py:340
  118.1 0.0 copy-start.2
  118.2 1.4 %copy.15 = bf16[24,1024]{1,0:T(8,128)(2,1)} copy(bf16[24,1024]{1,0:T(8,128)(2,1)} %get-tuple-element.10) | data formatting | bytes 98304
  119.6 0.0 copy-done.2
  119.6 0.6 copy.16
  120.2 0.0 copy-start.1
  120.2 2.4 %copy.17 = f32[1024,256]{1,0:T(8,128)} copy(f32[1024,256]{1,0:T(8,128)} %get-tuple-element.12) | data formatting | bytes 2097152
  122.6 0.0 copy-done.1
  122.6 0.0 copy-start
  122.6 1.0 copy.18
  123.5 0.6 copy-done
  124.2 1.0 copy.19
Async XLA Ops:
  118.1 1.4 %copy-start.2 = (bf16[24,1024]{1,0:T(8,128)(2,1)S(1)}, bf16[24,1024]{1,0:T(8,128)(2,1)}, u32[]{:S(2)}) copy-start(bf16[24,1024]{1,0:T(8,128)(2,1)} %get-tuple-element.11) | copy-start | bytes 147460
  120.2 2.4 %copy-start.1 = (f32[1024,256]{1,0:T(8,128)S(1)}, f32[1024,256]{1,0:T(8,128)}, u32[]{:S(2)}) copy-start(f32[1024,256]{1,0:T(8,128)} %get-tuple-element.13) | copy-start | bytes 3145732
  122.6 1.6 %copy-start = (f32[1024,256]{1,0:T(8,128)S(1)}, f32[1024,256]{1,0:T(8,128)}, u32[]{:S(2)}) copy-start(f32[1024,256]{1,0:T(8,128)} %get-tuple-element.14) | copy-start | bytes 3145732

commit v2 on v1

--- a/solution.py
+++ b/solution.py
@@ -15,11 +15,9 @@
 
 def chunk_place(k):
     pair, odd = k // 2, k % 2
-    first = 1 - (pair + 2) // 3
-    last = pair // 3
-    third = pair // 2 - last
-    dzh = first * odd + third + last * (1 - odd)
-    dy = (1 - first - last) * (1 + 2 * odd) + 2 * last
+    late, last = pair // 2, pair // 3
+    dzh = (1 - late) * odd + late - last
+    dy = late * (3 - odd) + (pair + 2) // 3 - late
     return dzh, dy
 
 
@@ -46,7 +44,8 @@
     x, zh, y, c = gx // 2, gx % 2, gy // 2, gy % 2
     units = wg.shape[1]
     feats = wg.shape[0]
-    rows = gath.shape[2] * gath.shape[3]
+    block = gath.shape[3]
+    rows = 4 * block
 
     def at(x_, zh_, y_, c_, zl_):
         return (x_ * 2 + zh_, y_ * 2 + c_, zl_)
@@ -75,6 +74,9 @@
         dzh, dy = chunk_place(k)
         return ((zh + dzh) % 2) * 4 + (y + dy) % 4
 
+    def column(j):
+        return (x + j) % 4
+
     def core_copy():
         return send(mine, theirs, cx, (0,), core_peer)
 
@@ -85,20 +87,22 @@
         place = ((zh + dzh) % 2) * 4 + y
         return send(gath.at[c, place, owner], gath.at[c, place, owner], xa, (dzh, j - 1), x_peer(-j))
 
-    def gather_y(k, place, dy):
-        return send(gath.at[c, place], gath.at[c, place], ya, (k,), y_peer(4 - dy))
-
-    def forward(k, which):
-        return send(gath.at[which, slot(k)], gath.at[which, slot(k)], fw, (k,), core_peer)
-
-    def to_pair(k):
-        return send(zsend.at[k], zin1.at[k], z1, (k,), pair_peer)
-
-    def to_mid(k):
-        return send(zsend.at[k], zin2.at[k], z2, (k,), mid_peer)
-
-    def to_end(k):
-        return send(res.at[k], res.at[k], z3, (k,), pair_peer)
+    def gather_y(k, j, place, dy):
+        b = column(j)
+        return send(gath.at[c, place, b], gath.at[c, place, b], ya, (k, j), y_peer(4 - dy))
+
+    def forward(k, b, which):
+        s = slot(k)
+        return send(gath.at[which, s, b], gath.at[which, s, b], fw, (k, b), core_peer)
+
+    def to_pair(k, b):
+        return send(zsend.at[k, b], zin1.at[k, b], z1, (k, b), pair_peer)
+
+    def to_mid(k, b):
+        return send(zsend.at[k, b], zin2.at[k, b], z2, (k, b), mid_peer)
+
+    def to_end(k, b):
+        return send(res.at[k, b], res.at[k, b], z3, (k, b), pair_peer)
 
     def to_core(k):
         return send(both.at[k, 1 - c], cin.at[k], co, (k,), core_peer)
@@ -135,91 +139,183 @@
     core_copy().wait_recv()
     m, t = mine[...].astype(F32), theirs[...].astype(F32)
     half = m.shape[0] // 2
-    lo = jnp.where(c == 0, m[:half], t[half:])
-    hi = jnp.where(c == 0, t[:half], m[half:])
     own = zh * 4 + y
     other = (1 - zh) * 4 + y
-    gath[c, own, x] = jnp.concatenate([lo, hi], axis=0).astype(BF16)
+    for n in range(2):
+        mh, th = m[n * half:(n + 1) * half], t[n * half:(n + 1) * half]
+        lo = jnp.where(c == 0, mh, th)
+        hi = jnp.where(c == 0, th, mh)
+        gath[n, own, x] = jnp.concatenate([lo, hi], axis=0).astype(BF16)
+
+    def gather_send(k, j):
+        dzh, dy = chunk_place(k)
+        gather_y(k, j, ((zh + dzh) % 2) * 4 + y, dy).start()
+
     half_copy(own).start()
-    for j in (1, 3, 2):
+    for j in (1, 3):
         gather_x(0, j, x).start()
-    d_gate[...] = jnp.zeros_like(d_gate)
-    d_up[...] = jnp.zeros_like(d_up)
-    d_down[...] = jnp.zeros_like(d_down)
+    for k in (2, 6):
+        gather_send(k, 0)
+    gather_x(0, 2, x).start()
+    gather_send(7, 0)
     for cp in weight_copies:
         cp.wait()
-    for j in (1, 3, 2):
-        gather_x(0, j, (x + j) % 4).wait_recv()
-    forward(0, c).start()
-
-    def gather_send(k):
-        dzh, dy = chunk_place(k)
-        gather_y(k, ((zh + dzh) % 2) * 4 + y, dy).start()
-
-    gather_send(2)
-    gather_send(3)
+    for d in (d_gate, d_up, d_down):
+        d[...] = jnp.zeros_like(d)
+
+    def block_partial(k, b):
+        s = slot(k)
+        for n, w in enumerate((wg, wu, wd)):
+            p = dot_nn(gath[n // 2, s, b], w[...])
+            part[k, b, n] = p
+            zsend[k, b, n] = p.astype(BF16)
+
+        @pl.when(is_end)
+        def _():
+            to_pair(k, b).start()
+
+    def first_pass(k, j):
+        if k == 0:
+            gather_x(0, j, column(j)).wait_recv()
+        else:
+            gather_y(k, j, slot(k), 0).wait_recv()
+        forward(k, column(j), c).start()
+
+    def first_work(k, j):
+        forward(k, column(j), 1 - c).wait_recv()
+        block_partial(k, column(j))
+
+    near, far = ((0, 1), (0, 3), (2, 0), (6, 0)), ((0, 2), (7, 0))
+    early = ((0, 0),) + near + far
+    block_partial(0, x)
+    for k, j in near:
+        first_pass(k, j)
+    for j in (1, 3):
+        gather_send(2, j)
+        gather_send(6, j)
+    for k, j in near:
+        first_work(k, j)
+    for k, j in far:
+        first_pass(k, j)
+    gather_send(2, 2)
+    gather_send(6, 2)
+    for k, j in far:
+        first_work(k, j)
+    def late(k, j):
+        dzh, _ = chunk_place(k)
+        return (dzh == 1) | (j != 0)
+
+    def each_late(k, fn):
+        for b in range(4):
+            pl.when(late(k, b - x))(lambda: fn(b))
 
     def stage_partial(k):
-        forward(k, 1 - c).wait_recv()
+        each_late(k, lambda b: forward(k, b, 1 - c).wait_recv())
         s = slot(k)
         xs = gath[0, s].reshape(rows, feats)
         ys = gath[1, s].reshape(rows, feats)
-        for n, (a, w) in enumerate(((xs, wg), (xs, wu), (ys, wd))):
-            p = dot_nn(a, w[...])
-            part[k, n] = p
-            zsend[k, n] = p.astype(BF16)
-
-        @pl.when(is_end)
-        def _():
-            to_pair(k).start()
+        p = [dot_nn(a, w[...]) for a, w in ((xs, wg), (xs, wu), (ys, wd))]
+
+        def keep(b):
+            for n in range(3):
+                q = p[n][b * block:(b + 1) * block]
+                part[k, b, n] = q
+                zsend[k, b, n] = q.astype(BF16)
+
+            @pl.when(is_end)
+            def _():
+                to_pair(k, b).start()
+
+        each_late(k, keep)
 
     def stage_forward(k):
         @pl.when(k == 1)
         def _():
-            half_copy(other).wait_recv()
             for j in (1, 3, 2):
-                gather_x(1, j, x).start()
+                gather_x(1, j, column(j)).wait_recv()
+                forward(k, column(j), c).start()
             for j in (1, 3, 2):
-                gather_x(1, j, (x + j) % 4).wait_recv()
+                gather_send(3, j)
+                gather_send(4, j)
 
         @pl.when(k >= 2)
         def _():
-            gather_y(k, slot(k), 0).wait_recv()
-
-        forward(k, c).start()
-
-    def stage_pair(k):
-        to_pair(k).wait_recv()
+            for j in (0, 1, 3, 2):
+                @pl.when(late(k, j))
+                def _():
+                    gather_y(k, j, slot(k), 0).wait_recv()
+                    forward(k, column(j), c).start()
+
+        @pl.when(k == 3)
+        def _():
+            for j in (1, 3, 2):
+                gather_send(5, j)
+                gather_send(7, j)
+
+    def pair_block(k, b):
+        to_pair(k, b).wait_recv()
         for n in range(3):
-            a = part[k, n] + zin1[k, n].astype(F32)
-            part[k, n] = a
-            zsend[k, n] = a.astype(BF16)
-        to_mid(k).start()
-
-    def stage_units(k):
-        to_mid(k).wait_recv()
-        g = part[k, 0] + zin2[k, 0].astype(F32)
-        u = part[k, 1] + zin2[k, 1].astype(F32)
-        h = part[k, 2] + zin2[k, 2].astype(F32)
+            a = part[k, b, n] + zin1[k, b, n].astype(F32)
+            part[k, b, n] = a
+            zsend[k, b, n] = a.astype(BF16)
+        to_mid(k, b).start()
+
+    def units_block(k, b):
+        to_mid(k, b).wait_recv()
+        g, u, h = [part[k, b, n] + zin2[k, b, n].astype(F32) for n in range(3)]
         sig = 1.0 / (1.0 + jnp.exp(-g))
         silu = g * sig
-        res[k, 0] = (silu * u).astype(BF16)
-        res[k, 1] = (h * u * sig * (1.0 + g * (1.0 - sig))).astype(BF16)
-        res[k, 2] = (h * silu).astype(BF16)
-        to_end(k).start()
+        res[k, b, 0] = (silu * u).astype(BF16)
+        res[k, b, 1] = (h * u * sig * (1.0 + g * (1.0 - sig))).astype(BF16)
+        res[k, b, 2] = (h * silu).astype(BF16)
+        to_end(k, b).start()
+
+    def take(*work):
+        for fn, (k, j) in work:
+            fn(k, column(j))
+
+    first = early
+
+    def stage_mid(i):
+        @pl.when(i == 1)
+        def _():
+            for n in (4, 5, 6):
+                take((pair_block, first[n]), (units_block, first[n - 3]))
+
+        @pl.when(i == 2)
+        def _():
+            for n in (4, 5, 6):
+                pair_block(1, n - 4)
+                take((units_block, first[n]))
+            pair_block(1, 3)
+
+        @pl.when(i >= 3)
+        def _():
+            for b in range(4):
+                @pl.when((i <= CHUNKS) & late(i - 1, b - x))
+                def _():
+                    pair_block(i - 1, b)
+
+                @pl.when((i <= CHUNKS + 1) & late(i - 2, b - x))
+                def _():
+                    units_block(i - 2, b)
+
+    def results(k):
+        return [res[k, :, n].reshape(rows, units) for n in range(3)]
 
     def stage_project(k):
         @pl.when(is_end)
         def _():
-            to_end(k).wait_recv()
-
-        hid, gg, ug = res[k, 0], res[k, 1], res[k, 2]
+            for b in range(4):
+                to_end(k, b).wait_recv()
+
+        hid, gg, ug = results(k)
         both[k, 0] = dot_nt(hid, wd[...]).astype(BF16).reshape(both.shape[2:])
         both[k, 1] = (dot_nt(gg, wg[...]) + dot_nt(ug, wu[...])).astype(BF16).reshape(both.shape[2:])
         to_core(k).start()
 
     def stage_weights(k):
-        hid, gg, ug = res[k, 0], res[k, 1], res[k, 2]
+        hid, gg, ug = results(k)
         s = slot(k)
         xs = gath[0, s].reshape(rows, feats)
         ys = gath[1, s].reshape(rows, feats)
@@ -245,33 +341,46 @@
         def _():
             scatter_y(k).start()
 
+    @pl.when(is_mid)
+    def _():
+        take((pair_block, first[0]))
+
+    half_copy(other).wait_recv()
+    forward(1, x, c).start()
+    for j in (1, 3, 2):
+        gather_x(1, j, x).start()
+    for k in (3, 4, 5):
+        gather_send(k, 0)
+
+    @pl.when(is_mid)
+    def _():
+        take((units_block, first[0]))
+        for n in (1, 2, 3):
+            take((pair_block, first[n]))
+
+    stage_forward(1)
+
     def step(i, _):
         def when(k, fn, cond=None):
             ok = (k >= 0) & (k < CHUNKS)
             pl.when(ok if cond is None else ok & cond)(lambda: fn(k))
 
-        when(i - 9, stage_x)
-        when(i - 7, stage_core)
-        when(i - 6, stage_project)
-        when(i - 4, stage_units, is_mid)
-        when(i - 2, stage_pair, is_mid)
+        pl.when(is_mid)(lambda: stage_mid(i))
         when(i, stage_partial)
         when(i + 1, stage_forward)
-
-        @pl.when(i == 0)
-        def _():
-            gather_send(4)
-            gather_send(5)
-
-        @pl.when(i == 2)
-        def _():
-            gather_send(6)
-            gather_send(7)
-
-        when(i - 6, stage_weights)
+        when(i - 7, stage_x)
+        when(i - 5, stage_core)
+        when(i - 4, stage_project)
+        when(i - 4, stage_weights)
         return 0
 
-    lax.fori_loop(0, CHUNKS + 9, step, 0)
+    lax.fori_loop(1, CHUNKS + 3, step, 0)
+    stage_x(4)
+    stage_core(6)
+    stage_x(5)
+    stage_project(7)
+    stage_weights(7)
+    stage_core(7)
 
     def total(first, others):
         s = ysend[first].astype(F32)
@@ -280,9 +389,11 @@
             s += yin[k].astype(F32)
         return s
 
-    zhs[...] = total(1, (4, 5, 6)).astype(BF16)
+    stage_x(6)
+    zhs[...] = total(1, (3, 4, 5)).astype(BF16)
     half_back().start()
-    s = total(0, (2, 3, 7))
+    stage_x(7)
+    s = total(0, (2, 6, 7))
     half_back().wait_recv()
     s += zhin[...].astype(F32)
     fin[...] = (gath[c, own, x].astype(F32) + s).astype(BF16)
@@ -303,19 +414,23 @@
     def drain(k, _):
         @pl.when(k >= 2)
         def _():
-            gather_y(k, slot(k), 0).wait_send()
+            for j in range(4):
+                gather_y(k, j, slot(k), 0).wait_send()
             scatter_y(k).wait_send()
 
-        forward(k, c).wait_send()
-
-        @pl.when(is_end)
-        def _():
-            to_pair(k).wait_send()
-
-        @pl.when(is_mid)
-        def _():
-            to_mid(k).wait_send()
-            to_end(k).wait_send()
+        for b in range(4):
+            @pl.when((k != 0) | (b != x))
+            def _():
+                forward(k, b, c).wait_send()
+
+            @pl.when(is_end)
+            def _():
+                to_pair(k, b).wait_send()
+
+            @pl.when(is_mid)
+            def _():
+                to_mid(k, b).wait_send()
+                to_end(k, b).wait_send()
 
         to_core(k).wait_send()
         for j in (1, 2, 3):
@@ -352,11 +467,11 @@
             vm(wshape, BF16), vm(wshape, BF16), vm(wshape, BF16),
             vm((block, feats), BF16), vm((block, feats), BF16),
             vm((2, CHUNKS, 4, block, feats), BF16),
-            vm((CHUNKS, 3, rows, units), F32),
-            vm((CHUNKS, 3, rows, units), BF16),
-            vm((CHUNKS, 3, rows, units), BF16),
-            vm((CHUNKS, 3, rows, units), BF16),
-            vm((CHUNKS, 3, rows, units), BF16),
+            vm((CHUNKS, 4, 3, block, units), F32),
+            vm((CHUNKS, 4, 3, block, units), BF16),
+            vm((CHUNKS, 4, 3, block, units), BF16),
+            vm((CHUNKS, 4, 3, block, units), BF16),
+            vm((CHUNKS, 4, 3, block, units), BF16),
             vm((CHUNKS, 2, 4, block, feats), BF16),
             vm((CHUNKS, 4, block, feats), BF16),
             vm((CHUNKS, 4, block, feats), BF16),
@@ -366,8 +481,8 @@
             vm((block, feats), BF16), vm((block, feats), BF16),
             vm((block, feats), BF16), vm((block, feats), BF16),
             dma((3,)),
-            dma((2, 1)), dma((2, 1)), dma((2, 2, 3)), dma((2, CHUNKS)), dma((2, CHUNKS)),
-            dma((2, CHUNKS)), dma((2, CHUNKS)), dma((2, CHUNKS)), dma((2, CHUNKS)),
+            dma((2, 1)), dma((2, 1)), dma((2, 2, 3)), dma((2, CHUNKS, 4)), dma((2, CHUNKS, 4)),
+            dma((2, CHUNKS, 4)), dma((2, CHUNKS, 4)), dma((2, CHUNKS, 4)), dma((2, CHUNKS)),
             dma((2, CHUNKS, 3)), dma((2, CHUNKS)), dma((2, 1)), dma((2, 1)),
         ],
         compiler_params=pltpu.CompilerParams(

time: 125 us -> 116 us (0.928)
  the two profiles are of different devices: /device:TPU:1 before, /device:TPU:33 now
where the time goes in v2:
time: 116 us
  Pallas kernels  108 us (93%)
  local copies, waits for them, and re-layouts  6.98 us (6%)
    pallas_call x1, Pallas kernels, on_device(): pl.pallas_call(body, out_shape=(jax.ShapeDtypeStruct(tokens.shape, BF16),...  108 us
    unnamed x11, local copies, waits for them, and re-layouts  6.98 us

profile of v2, /device:TPU:33, one launch (start us, length us, event | category | flops | bytes accessed | tf_op | source)
XLA Modules:
  0.0 115.7 jit_solution(6205709010113767707)
XLA Ops:
  0.6 108.1 %swiglu_block.1 = (bf16[24,1024]{1,0:T(8,128)(2,1)}, bf16[24,1024]{1,0:T(8,128)(2,1)}, f32[1024,256]{1,0:T(8,128)}, f32[1024,256]{1,0:T(8,128)}, f32[1024,256]{1,0:T(8,128)}) custom-call(bf16[24,1024]{1,0:T(8,128)(2,1)} %tok.1, bf16[24,1024]{1,0:T(8,128)(2,1)} %grd.1, bf16[1024,256]{1,0:T(8,128)(2,1)} %wg_any.1, bf16[1024,256]{1,0:T(8,128)(2,1)} %wu_any.1, ...), custom_call_target="tpu_custom_call" | custom-call | flops 7247757312 | bytes 5242880 | tf_op jit(solution)/shard_map/swiglu_block/pallas_call | solution.py:455
  108.7 0.0 copy-start.2
  108.7 1.4 %copy.15 = bf16[24,1024]{1,0:T(8,128)(2,1)} copy(bf16[24,1024]{1,0:T(8,128)(2,1)} %get-tuple-element.10) | data formatting | bytes 98304
  110.1 0.0 copy-done.2
  110.2 0.6 copy.16
  110.8 0.0 copy-start.1
  110.8 2.4 %copy.17 = f32[1024,256]{1,0:T(8,128)} copy(f32[1024,256]{1,0:T(8,128)} %get-tuple-element.12) | data formatting | bytes 2097152
  113.1 0.0 copy-done.1
  113.1 0.0 copy-start
  113.1 1.0 copy.18
  114.1 0.6 copy-done
  114.7 1.0 copy.19
Async XLA Ops:
  108.7 1.4 %copy-start.2 = (bf16[24,1024]{1,0:T(8,128)(2,1)S(1)}, bf16[24,1024]{1,0:T(8,128)(2,1)}, u32[]{:S(2)}) copy-start(bf16[24,1024]{1,0:T(8,128)(2,1)} %get-tuple-element.11) | copy-start | bytes 147460
  110.8 2.4 %copy-start.1 = (f32[1024,256]{1,0:T(8,128)S(1)}, f32[1024,256]{1,0:T(8,128)}, u32[]{:S(2)}) copy-start(f32[1024,256]{1,0:T(8,128)} %get-tuple-element.13) | copy-start | bytes 3145732
  113.1 1.6 %copy-start = (f32[1024,256]{1,0:T(8,128)S(1)}, f32[1024,256]{1,0:T(8,128)}, u32[]{:S(2)}) copy-start(f32[1024,256]{1,0:T(8,128)} %get-tuple-element.14) | copy-start | bytes 3145732

commit v3 on v2

--- a/solution.py
+++ b/solution.py
@@ -11,6 +11,7 @@
 F32 = jnp.float32
 BF16 = jnp.bfloat16
 CHUNKS = 8
+LAST_OWN = (1, 3, 2, 0)
 
 
 def chunk_place(k):
@@ -25,20 +26,16 @@
     return jnp.dot(a, b, preferred_element_type=F32)
 
 
-def dot_nt(a, b):
-    return lax.dot_general(a, b, (((1,), (1,)), ((), ())), preferred_element_type=F32)
-
-
 def dot_tn(a, b):
     return lax.dot_general(a, b, (((0,), (0,)), ((), ())), preferred_element_type=F32)
 
 
 def body(
-    tok, grd, wg_any, wu_any, wd_any,
+    tok_any, grd_any, wg_any, wu_any, wd_any,
     out, gtok, d_gate, d_up, d_down,
-    wg, wu, wd, mine, theirs, gath, part, zsend, zin1, zin2, res,
+    tok, grd, wg, wu, wd, wgt, wut, wdt, mine, theirs, gath, part, zsend, zin1, zin2, res,
     both, cin, xsend, xin, ysend, yin, zhs, zhin, fin, fin_in,
-    w_sem, cx, zx, xa, ya, fw, z1, z2, z3, co, xr, yr, zr, fo,
+    w_sem, cx, zx, xa, ya, fw, z1, z2, z3, co, cl, xr, yr, zr, fo,
 ):
     gx, gy, zl = lax.axis_index("gx"), lax.axis_index("gy"), lax.axis_index("gz")
     x, zh, y, c = gx // 2, gx % 2, gy // 2, gy % 2
@@ -107,6 +104,9 @@
     def to_core(k):
         return send(both.at[k, 1 - c], cin.at[k], co, (k,), core_peer)
 
+    def last_core(b):
+        return send(both.at[CHUNKS - 1, 1 - c, b], cin.at[CHUNKS - 1, b], cl, (b,), core_peer)
+
     def scatter_x(k, j):
         return send(xsend.at[k, (x + j) % 4], xin.at[k, j - 1], xr, (k, j - 1), x_peer(j))
 
@@ -124,7 +124,8 @@
         pltpu.make_async_copy(src, dst, w_sem.at[n])
         for n, (src, dst) in enumerate(((wg_any, wg), (wu_any, wu), (wd_any, wd)))
     ]
-    for cp in weight_copies:
+    row_copies = [pltpu.make_async_copy(tok_any, tok, w_sem.at[3]), pltpu.make_async_copy(grd_any, grd, w_sem.at[4])]
+    for cp in row_copies + weight_copies:
         cp.start()
 
     peers = [core_peer, half_peer, pair_peer, mid_peer]
@@ -132,6 +133,8 @@
     barrier = pltpu.get_barrier_semaphore()
     for peer in peers:
         pl.semaphore_signal(barrier, inc=1, device_id=peer, device_id_type=MESH)
+    for cp in row_copies:
+        cp.wait()
     mine[...] = jnp.concatenate([tok[...].astype(F32), grd[...].astype(F32)], axis=0).astype(BF16)
     pl.semaphore_wait(barrier, len(peers))
 
@@ -157,7 +160,6 @@
     for k in (2, 6):
         gather_send(k, 0)
     gather_x(0, 2, x).start()
-    gather_send(7, 0)
     for cp in weight_copies:
         cp.wait()
     for d in (d_gate, d_up, d_down):
@@ -185,9 +187,11 @@
         forward(k, column(j), 1 - c).wait_recv()
         block_partial(k, column(j))
 
-    near, far = ((0, 1), (0, 3), (2, 0), (6, 0)), ((0, 2), (7, 0))
+    near, far = ((0, 1), (0, 3), (2, 0), (6, 0)), ((0, 2),)
     early = ((0, 0),) + near + far
     block_partial(0, x)
+    for flat, turned in ((wg, wgt), (wu, wut), (wd, wdt)):
+        turned[...] = flat[...].T
     for k, j in near:
         first_pass(k, j)
     for j in (1, 3):
@@ -203,11 +207,11 @@
         first_work(k, j)
     def late(k, j):
         dzh, _ = chunk_place(k)
-        return (dzh == 1) | (j != 0)
+        return (dzh == 1) | (j != 0) | (k == CHUNKS - 1)
 
     def each_late(k, fn):
-        for b in range(4):
-            pl.when(late(k, b - x))(lambda: fn(b))
+        for j in LAST_OWN:
+            pl.when(late(k, j))(lambda: fn(column(j)))
 
     def stage_partial(k):
         each_late(k, lambda b: forward(k, b, 1 - c).wait_recv())
@@ -216,17 +220,17 @@
         ys = gath[1, s].reshape(rows, feats)
         p = [dot_nn(a, w[...]) for a, w in ((xs, wg), (xs, wu), (ys, wd))]
 
-        def keep(b):
-            for n in range(3):
-                q = p[n][b * block:(b + 1) * block]
-                part[k, b, n] = q
-                zsend[k, b, n] = q.astype(BF16)
-
-            @pl.when(is_end)
+        for b in range(4):
+            @pl.when(late(k, b - x))
             def _():
-                to_pair(k, b).start()
-
-        each_late(k, keep)
+                for n in range(3):
+                    q = p[n][b * block:(b + 1) * block]
+                    part[k, b, n] = q
+                    zsend[k, b, n] = q.astype(BF16)
+
+        @pl.when(is_end)
+        def _():
+            each_late(k, lambda b: to_pair(k, b).start())
 
     def stage_forward(k):
         @pl.when(k == 1)
@@ -240,7 +244,7 @@
 
         @pl.when(k >= 2)
         def _():
-            for j in (0, 1, 3, 2):
+            for j in LAST_OWN:
                 @pl.when(late(k, j))
                 def _():
                     gather_y(k, j, slot(k), 0).wait_recv()
@@ -248,8 +252,9 @@
 
         @pl.when(k == 3)
         def _():
-            for j in (1, 3, 2):
-                gather_send(5, j)
+            for j in LAST_OWN:
+                if j:
+                    gather_send(5, j)
                 gather_send(7, j)
 
     def pair_block(k, b):
@@ -279,26 +284,25 @@
     def stage_mid(i):
         @pl.when(i == 1)
         def _():
-            for n in (4, 5, 6):
+            for n in (4, 5):
                 take((pair_block, first[n]), (units_block, first[n - 3]))
 
         @pl.when(i == 2)
         def _():
-            for n in (4, 5, 6):
-                pair_block(1, n - 4)
-                take((units_block, first[n]))
-            pair_block(1, 3)
+            for n in (3, 4, 5):
+                take((pair_block, (1, LAST_OWN[n - 3])), (units_block, first[n]))
+            take((pair_block, (1, LAST_OWN[3])))
 
         @pl.when(i >= 3)
         def _():
-            for b in range(4):
-                @pl.when((i <= CHUNKS) & late(i - 1, b - x))
+            for j in LAST_OWN:
+                @pl.when((i <= CHUNKS) & late(i - 1, j))
                 def _():
-                    pair_block(i - 1, b)
-
-                @pl.when((i <= CHUNKS + 1) & late(i - 2, b - x))
+                    pair_block(i - 1, column(j))
+
+                @pl.when((i <= CHUNKS + 1) & late(i - 2, j))
                 def _():
-                    units_block(i - 2, b)
+                    units_block(i - 2, column(j))
 
     def results(k):
         return [res[k, :, n].reshape(rows, units) for n in range(3)]
@@ -310,8 +314,8 @@
                 to_end(k, b).wait_recv()
 
         hid, gg, ug = results(k)
-        both[k, 0] = dot_nt(hid, wd[...]).astype(BF16).reshape(both.shape[2:])
-        both[k, 1] = (dot_nt(gg, wg[...]) + dot_nt(ug, wu[...])).astype(BF16).reshape(both.shape[2:])
+        both[k, 0] = dot_nn(hid, wdt[...]).astype(BF16).reshape(both.shape[2:])
+        both[k, 1] = (dot_nn(gg, wgt[...]) + dot_nn(ug, wut[...])).astype(BF16).reshape(both.shape[2:])
         to_core(k).start()
 
     def stage_weights(k):
@@ -375,13 +379,6 @@
         return 0
 
     lax.fori_loop(1, CHUNKS + 3, step, 0)
-    stage_x(4)
-    stage_core(6)
-    stage_x(5)
-    stage_project(7)
-    stage_weights(7)
-    stage_core(7)
-
     def total(first, others):
         s = ysend[first].astype(F32)
         for k in others:
@@ -389,10 +386,43 @@
             s += yin[k].astype(F32)
         return s
 
+    end = CHUNKS - 1
+
+    def last_project(j):
+        b = column(j)
+
+        @pl.when(is_end)
+        def _():
+            to_end(end, b).wait_recv()
+
+        hid, gg, ug = res[end, b, 0], res[end, b, 1], res[end, b, 2]
+        both[end, 0, b] = dot_nn(hid, wdt[...]).astype(BF16)
+        both[end, 1, b] = (dot_nn(gg, wgt[...]) + dot_nn(ug, wut[...])).astype(BF16)
+        last_core(b).start()
+
+    def last_scatter(j):
+        b = column(j)
+        last_core(b).wait_recv()
+        xsend[end, b] = (both[end, c, b].astype(F32) + cin[end, b].astype(F32)).astype(BF16)
+        if j:
+            scatter_x(end, j).start()
+
+    stage_core(6)
+    stage_x(4)
+    last_project(1)
+    last_project(3)
+    last_scatter(1)
+    stage_x(5)
+    last_project(2)
+    last_scatter(3)
+    last_project(0)
+    last_scatter(2)
+    last_scatter(0)
     stage_x(6)
     zhs[...] = total(1, (3, 4, 5)).astype(BF16)
     half_back().start()
-    stage_x(7)
+    stage_x(end)
+    stage_weights(end)
     s = total(0, (2, 6, 7))
     half_back().wait_recv()
     s += zhin[...].astype(F32)
@@ -432,14 +462,29 @@
                 to_mid(k, b).wait_send()
                 to_end(k, b).wait_send()
 
-        to_core(k).wait_send()
+        @pl.when(k < CHUNKS - 1)
+        def _():
+            to_core(k).wait_send()
+
         for j in (1, 2, 3):
             scatter_x(k, j).wait_send()
         return 0
 
     lax.fori_loop(0, CHUNKS, drain, 0)
+    for b in range(4):
+        last_core(b).wait_send()
     half_back().wait_send()
     last_copy().wait_send()
+
+
+def hand_over(*refs):
+    n = (len(refs) - 1) // 2
+    sems = refs[-1]
+    copies = [pltpu.make_async_copy(refs[i], refs[n + i], sems.at[i]) for i in range(n)]
+    for cp in copies:
+        cp.start()
+    for cp in copies:
+        cp.wait()
 
 
 def on_device(tokens, gate_weight, up_weight, down_weight, grad_out):
@@ -450,21 +495,18 @@
     dma = pltpu.SemaphoreType.DMA
     vm = pltpu.VMEM
     wshape = (feats, units)
+    outs = [(tokens.shape, BF16)] * 2 + [(wshape, F32)] * 3
     any_spec = pl.BlockSpec(memory_space=pl.ANY)
     vmem_spec = pl.BlockSpec(memory_space=pltpu.VMEM)
-    return pl.pallas_call(
+    made = pl.pallas_call(
         body,
-        out_shape=(
-            jax.ShapeDtypeStruct(tokens.shape, BF16),
-            jax.ShapeDtypeStruct(tokens.shape, BF16),
-            jax.ShapeDtypeStruct(wshape, F32),
-            jax.ShapeDtypeStruct(wshape, F32),
-            jax.ShapeDtypeStruct(wshape, F32),
-        ),
-        in_specs=[vmem_spec, vmem_spec, any_spec, any_spec, any_spec],
+        out_shape=[vm(sh, dt) for sh, dt in outs],
+        in_specs=[pl.BlockSpec(memory_space=pltpu.HBM)] * 5,
         out_specs=[vmem_spec] * 5,
         scratch_shapes=[
+            vm(tokens.shape, BF16), vm(tokens.shape, BF16),
             vm(wshape, BF16), vm(wshape, BF16), vm(wshape, BF16),
+            vm(wshape[::-1], BF16), vm(wshape[::-1], BF16), vm(wshape[::-1], BF16),
             vm((block, feats), BF16), vm((block, feats), BF16),
             vm((2, CHUNKS, 4, block, feats), BF16),
             vm((CHUNKS, 4, 3, block, units), F32),
@@ -480,13 +522,13 @@
             vm((CHUNKS, block, feats), BF16),
             vm((block, feats), BF16), vm((block, feats), BF16),
             vm((block, feats), BF16), vm((block, feats), BF16),
-            dma((3,)),
+            dma((5,)),
             dma((2, 1)), dma((2, 1)), dma((2, 2, 3)), dma((2, CHUNKS, 4)), dma((2, CHUNKS, 4)),
             dma((2, CHUNKS, 4)), dma((2, CHUNKS, 4)), dma((2, CHUNKS, 4)), dma((2, CHUNKS)),
-            dma((2, CHUNKS, 3)), dma((2, CHUNKS)), dma((2, 1)), dma((2, 1)),
+            dma((2, 4)), dma((2, CHUNKS, 3)), dma((2, CHUNKS)), dma((2, 1)), dma((2, 1)),
         ],
         compiler_params=pltpu.CompilerParams(
-            collective_id=0, has_side_effects=True, vmem_limit_bytes=60 << 20
+            collective_id=0, has_side_effects=True, vmem_limit_bytes=46 << 20
         ),
         cost_estimate=pl.CostEstimate(
             flops=18 * 8 * rows * feats * units,
@@ -494,7 +536,19 @@
             bytes_accessed=20 * feats * units,
         ),
         name="swiglu_block",
-    )(tokens, grad_out, gate_weight, up_weight, down_weight)
+    )(*[
+        pltpu.with_memory_space_constraint(a, pltpu.HBM)
+        for a in (tokens, grad_out, gate_weight, up_weight, down_weight)
+    ])
+    return pl.pallas_call(
+        hand_over,
+        out_shape=[jax.ShapeDtypeStruct(sh, dt) for sh, dt in outs],
+        in_specs=[vmem_spec] * len(outs),
+        out_specs=[any_spec] * len(outs),
+        scratch_shapes=[dma((len(outs),))],
+        compiler_params=pltpu.CompilerParams(vmem_limit_bytes=1 << 20),
+        name="hand_over",
+    )(*made)
 
 
 def solution(mesh):

time: 116 us -> 107 us (0.922)
  local copies, waits for them, and re-layouts: 6.98 us -> 0 us
  Pallas kernels: 108 us -> 106 us
    unnamed x11 -> x0, local copies, waits for them, and re-layouts: 6.98 us -> none
    pallas_call x1 -> x2, Pallas kernels: 108 us -> 106 us  [the longest x1 105 us: on_device(): pl.pallas_call(body, out_shape=[vm(sh, dt) for sh, dt in outs], in_specs=...]
where the time goes in v3:
time: 107 us
  Pallas kernels  106 us (99%)
    pallas_call x1, Pallas kernels, on_device(): pl.pallas_call(body, out_shape=[vm(sh, dt) for sh, dt in outs], in_specs=...  105 us

profile of v3, /device:TPU:33, one launch (start us, length us, event | category | flops | bytes accessed | tf_op | source)
XLA Modules:
  0.0 106.9 jit_solution(8625285275679591903)
XLA Ops:
  0.6 104.5 %swiglu_block.1 = (bf16[24,1024]{1,0:T(8,128)(2,1)S(1)}, bf16[24,1024]{1,0:T(8,128)(2,1)S(1)}, f32[1024,256]{1,0:T(8,128)S(1)}, f32[1024,256]{1,0:T(8,128)S(1)}, f32[1024,256]{1,0:T(8,128)S(1)}) custom-call(bf16[24,1024]{1,0:T(8,128)(2,1)} %tok_any.1, bf16[24,1024]{1,0:T(8,128)(2,1)} %grd_any.1, bf16[1024,256]{1,0:T(8,128)(2,1)} %wg_any.1, ...), custom_call_target="tpu_custom_call" | custom-call | flops 7247757312 | bytes 5242880 | tf_op jit(solution)/shard_map/swiglu_block/pallas_call | solution.py:501
  105.1 1.7 %hand_over.1 = (bf16[24,1024]{1,0:T(8,128)(2,1)}, bf16[24,1024]{1,0:T(8,128)(2,1)}, f32[1024,256]{1,0:T(8,128)}, f32[1024,256]{1,0:T(8,128)}, f32[1024,256]{1,0:T(8,128)}) custom-call(bf16[24,1024]{1,0:T(8,128)(2,1)S(1)} %get-tuple-element.10.refs_0_, bf16[24,1024]{1,0:T(8,128)(2,1)S(1)} %get-tuple-element.11.refs_1_, ...), custom_call_target="tpu_custom_call" | custom-call | tf_op jit(solution)/shard_map/hand_over/pallas_call | solution.py:543

commit v4 on v3

--- a/solution.py
+++ b/solution.py
@@ -364,6 +364,8 @@
 
     stage_forward(1)
 
+    ahead = 2 * (((zl + 1) // 2) % 2)
+
     def step(i, _):
         def when(k, fn, cond=None):
             ok = (k >= 0) & (k < CHUNKS)
@@ -372,10 +374,11 @@
         pl.when(is_mid)(lambda: stage_mid(i))
         when(i, stage_partial)
         when(i + 1, stage_forward)
-        when(i - 7, stage_x)
-        when(i - 5, stage_core)
-        when(i - 4, stage_project)
-        when(i - 4, stage_weights)
+        k = i - 4 + ahead
+        when(k - 3, stage_x, k - 3 < CHUNKS - 2)
+        when(k - 1, stage_core, k - 1 < CHUNKS - 1)
+        when(k, stage_project, k < CHUNKS - 1)
+        when(k, stage_weights, k < CHUNKS - 2)
         return 0
 
     lax.fori_loop(1, CHUNKS + 3, step, 0)
@@ -407,12 +410,16 @@
         if j:
             scatter_x(end, j).start()
 
-    stage_core(6)
-    stage_x(4)
+
+    @pl.when(is_end)
+    def _():
+        stage_core(6)
+        stage_x(4)
+
     last_project(1)
     last_project(3)
     last_scatter(1)
-    stage_x(5)
+    pl.when(is_end)(lambda: stage_x(5))
     last_project(2)
     last_scatter(3)
     last_project(0)
@@ -422,6 +429,7 @@
     zhs[...] = total(1, (3, 4, 5)).astype(BF16)
     half_back().start()
     stage_x(end)
+    stage_weights(end - 1)
     stage_weights(end)
     s = total(0, (2, 6, 7))
     half_back().wait_recv()

time: 107 us -> 103 us (0.963)
  the two profiles are of different devices: /device:TPU:33 before, /device:TPU:1 now
where the time goes in v4:
time: 103 us
  Pallas kernels  102 us (99%)
    pallas_call x1, Pallas kernels, on_device(): pl.pallas_call(body, out_shape=[vm(sh, dt) for sh, dt in outs], in_specs=...  101 us

profile of v4, /device:TPU:1, one launch (start us, length us, event | category | flops | bytes accessed | tf_op | source)
XLA Modules:
  0.0 103.0 jit_solution(4649079226653776090)
XLA Ops:
  0.6 100.6 %swiglu_block.1 = (bf16[24,1024]{1,0:T(8,128)(2,1)S(1)}, bf16[24,1024]{1,0:T(8,128)(2,1)S(1)}, f32[1024,256]{1,0:T(8,128)S(1)}, f32[1024,256]{1,0:T(8,128)S(1)}, f32[1024,256]{1,0:T(8,128)S(1)}) custom-call(bf16[24,1024]{1,0:T(8,128)(2,1)} %tok_any.1, bf16[24,1024]{1,0:T(8,128)(2,1)} %grd_any.1, bf16[1024,256]{1,0:T(8,128)(2,1)} %wg_any.1, ...), custom_call_target="tpu_custom_call" | custom-call | flops 7247757312 | bytes 5242880 | tf_op jit(solution)/shard_map/swiglu_block/pallas_call | solution.py:509
  101.2 1.7 %hand_over.1 = (bf16[24,1024]{1,0:T(8,128)(2,1)}, bf16[24,1024]{1,0:T(8,128)(2,1)}, f32[1024,256]{1,0:T(8,128)}, f32[1024,256]{1,0:T(8,128)}, f32[1024,256]{1,0:T(8,128)}) custom-call(bf16[24,1024]{1,0:T(8,128)(2,1)S(1)} %get-tuple-element.10.refs_0_, bf16[24,1024]{1,0:T(8,128)(2,1)S(1)} %get-tuple-element.11.refs_1_, ...), custom_call_target="tpu_custom_call" | custom-call | tf_op jit(solution)/shard_map/hand_over/pallas_call | solution.py:551

commit v5 on v4

--- a/solution.py
+++ b/solution.py
@@ -375,10 +375,10 @@
         when(i, stage_partial)
         when(i + 1, stage_forward)
         k = i - 4 + ahead
-        when(k - 3, stage_x, k - 3 < CHUNKS - 2)
+        when(k - 3, stage_x, k - 3 < CHUNKS - 3)
         when(k - 1, stage_core, k - 1 < CHUNKS - 1)
         when(k, stage_project, k < CHUNKS - 1)
-        when(k, stage_weights, k < CHUNKS - 2)
+        when(k - 1, stage_weights, k - 1 < CHUNKS - 4)
         return 0
 
     lax.fori_loop(1, CHUNKS + 3, step, 0)
@@ -419,7 +419,7 @@
     last_project(1)
     last_project(3)
     last_scatter(1)
-    pl.when(is_end)(lambda: stage_x(5))
+    stage_x(5)
     last_project(2)
     last_scatter(3)
     last_project(0)
@@ -429,8 +429,8 @@
     zhs[...] = total(1, (3, 4, 5)).astype(BF16)
     half_back().start()
     stage_x(end)
-    stage_weights(end - 1)
-    stage_weights(end)
+    for k in range(CHUNKS - 4, CHUNKS):
+        stage_weights(k)
     s = total(0, (2, 6, 7))
     half_back().wait_recv()
     s += zhin[...].astype(F32)

time: 103 us -> 103 us (level)
  no operation moved by 1% of the time
where the time goes in v5:
time: 103 us
  Pallas kernels  102 us (99%)
    pallas_call x1, Pallas kernels, on_device(): pl.pallas_call(body, out_shape=[vm(sh, dt) for sh, dt in outs], in_specs=...  100 us

profile of v5, /device:TPU:1, one launch (start us, length us, event | category | flops | bytes accessed | tf_op | source)
XLA Modules:
  0.0 102.7 jit_solution(13892035743498012791)
XLA Ops:
  0.6 100.3 %swiglu_block.1 = (bf16[24,1024]{1,0:T(8,128)(2,1)S(1)}, bf16[24,1024]{1,0:T(8,128)(2,1)S(1)}, f32[1024,256]{1,0:T(8,128)S(1)}, f32[1024,256]{1,0:T(8,128)S(1)}, f32[1024,256]{1,0:T(8,128)S(1)}) custom-call(bf16[24,1024]{1,0:T(8,128)(2,1)} %tok_any.1, bf16[24,1024]{1,0:T(8,128)(2,1)} %grd_any.1, bf16[1024,256]{1,0:T(8,128)(2,1)} %wg_any.1, ...), custom_call_target="tpu_custom_call" | custom-call | flops 7247757312 | bytes 5242880 | tf_op jit(solution)/shard_map/swiglu_block/pallas_call | solution.py:509
  100.9 1.7 %hand_over.1 = (bf16[24,1024]{1,0:T(8,128)(2,1)}, bf16[24,1024]{1,0:T(8,128)(2,1)}, f32[1024,256]{1,0:T(8,128)}, f32[1024,256]{1,0:T(8,128)}, f32[1024,256]{1,0:T(8,128)}) custom-call(bf16[24,1024]{1,0:T(8,128)(2,1)S(1)} %get-tuple-element.10.refs_0_, bf16[24,1024]{1,0:T(8,128)(2,1)S(1)} %get-tuple-element.11.refs_1_, ...), custom_call_target="tpu_custom_call" | custom-call | tf_op jit(solution)/shard_map/hand_over/pallas_call | solution.py:551
